TPU v7x, 32 devices: a whole 2x2x4 slice. The times are simulated.
32 devices in a mesh: dom: 2 (over y), bank: 2 (over core), grp: 8 (over z, x).
Axes of the slice: x: 2, y: 2, z: 4, core: 2. Of those that a mesh axis runs over, the one named last changes fastest.
Arguments:
- embeddings: bfloat16 [8192, 768], P(('dom', 'bank', 'grp')), parts along dimension 0
- cluster_of: int32 [8192], P(('dom', 'bank', 'grp')), parts along dimension 0, may hold values from 0 to 3, as said below
- dest_list: int32 [32, 16, 32], P(('dom', 'bank', 'grp')), parts along dimension 0, may hold values from -1 to 255, as said below
Outputs:
- best_sim: float32 [8192], P(('dom', 'bank', 'grp')), parts along dimension 0
There are 2 independent parts, one for each index of `dom`. A program takes and returns all parts, laid end to end along the dimension named above; each array names one. Nothing has to cross between parts.
Inputs may be any that keep to these rules, and one draw needn't show every extreme that they name: For each crawl shard s, each of its 256 local rows appears exactly once in dest_list[s]; in each list dest_list[s, d] the used slots come first and the rest hold -1; every destination device receives exactly 256 rows in all; in every draw some shard fills all 32 slots to some destination. A row's cluster lies in slab (cluster_of // 2), which equals the bank index of the device that dest_list sends the row to.
All inputs are finite; a program needn't handle non-finite values.
Results may differ from a plain program's by a relative error of at most 0.0025.
Values may be sent and summed in bfloat16 or wider, within the bound.
A program may use at most 128 MiB of HBM per device.

v0:
```python
import jax
import jax.numpy as jnp
from jax import lax
from jax.sharding import PartitionSpec as P

small_eps = 1e-06


def masked_scores(query_rows, query_cluster, other_rows, other_cluster):
    scores = lax.dot_general(
        query_rows, other_rows, (((1,), (1,)), ((), ())), preferred_element_type=jnp.float32
    )
    matching = query_cluster[:, None] == other_cluster[None, :]
    return (scores, matching)


def on_device(embeddings, cluster_of, dest_list):
    rows_dev = embeddings.shape[0]
    width = embeddings.shape[1]
    devices_part = dest_list.shape[1]
    capacity = dest_list.shape[2]
    source = lax.axis_index(("bank", "grp"))
    widened = embeddings.astype(jnp.float32)
    unit_rows = (
        widened * lax.rsqrt(jnp.sum(widened * widened, axis=1, keepdims=True) + small_eps)
    ).astype(jnp.bfloat16)
    slot_rows = dest_list[0]
    is_live = slot_rows >= 0
    safe_rows = jnp.where(is_live, slot_rows, 0)
    outgoing = jnp.take(unit_rows, safe_rows.reshape(-1), axis=0).reshape(
        devices_part, capacity, width
    )
    out_cluster = jnp.where(is_live, jnp.take(cluster_of, safe_rows), -1)
    out_crawl = jnp.where(is_live, source * rows_dev + safe_rows, -1)
    arrived, in_cluster, in_crawl = (
        lax.all_to_all(outgoing, ("bank", "grp"), split_axis=0, concat_axis=0, tiled=True),
        lax.all_to_all(out_cluster, ("bank", "grp"), split_axis=0, concat_axis=0, tiled=True),
        lax.all_to_all(out_crawl, ("bank", "grp"), split_axis=0, concat_axis=0, tiled=True),
    )
    flat_cluster = in_cluster.reshape(-1)
    flat_crawl = in_crawl.reshape(-1)
    present = flat_cluster >= 0
    position = jnp.cumsum(present.astype(jnp.int32)) - 1
    chosen = (position[None, :] == jnp.arange(rows_dev, dtype=jnp.int32)[:, None]) & present[
        None, :
    ]
    key_rows = jnp.dot(
        chosen.astype(jnp.bfloat16), arrived.reshape(-1, width), preferred_element_type=jnp.float32
    ).astype(jnp.bfloat16)
    key_cluster = jnp.sum(jnp.where(chosen, flat_cluster[None, :], 0), axis=1)
    key_crawl = jnp.sum(jnp.where(chosen, flat_crawl[None, :], 0), axis=1)
    floor_value = jnp.full((rows_dev,), -1.0, jnp.float32)
    scores, matching = masked_scores(
        key_rows,
        key_cluster,
        lax.all_gather(key_rows, "grp", axis=0, tiled=True),
        lax.all_gather(key_cluster, "grp", axis=0, tiled=True),
    )
    earlier = matching & (
        lax.all_gather(key_crawl, "grp", axis=0, tiled=True)[None, :] < key_crawl[:, None]
    )
    best_sim = jnp.maximum(floor_value, jnp.max(jnp.where(earlier, scores, -1.0), axis=1))
    slot_best = jnp.where(
        present, jnp.take(best_sim, jnp.clip(position, 0, rows_dev - 1)), -1.0
    ).reshape(devices_part, capacity)
    returned_best = lax.all_to_all(
        slot_best, ("bank", "grp"), split_axis=0, concat_axis=0, tiled=True
    )
    result = (
        jnp.full((rows_dev,), -1.0, jnp.float32)
        .at[safe_rows.reshape(-1)]
        .max(jnp.where(is_live, returned_best, -1.0).reshape(-1))
    )
    return result


def solution(mesh):
    return jax.shard_map(
        on_device,
        mesh=mesh,
        in_specs=(
            P(("dom", "bank", "grp"), None),
            P(("dom", "bank", "grp")),
            P(("dom", "bank", "grp"), None, None),
        ),
        out_specs=P(("dom", "bank", "grp")),
        check_vma=False,
    )
```

profile of v0, /device:TPU:1, one launch (start us, length us, event | category | flops | bytes accessed | tf_op | source)
XLA Modules:
  0.0 139.3 jit_solution(7772773882781475917)
XLA Ops:
  6.5 0.7 compare_select_fusion.4
  7.3 0.1 reshape.336
  7.4 0.0 copy-start.1
  7.4 3.5 %gather_fusion = s32[512]{0:T(512)S(1)} fusion(s32[256]{0:T(256)S(1)} %copy-done, s32[1024]{0:T(1024)S(1)} %pad_clamp_fusion.2), kind=kCustom, calls=%fused_computation | custom fusion | bytes 6144 | tf_op jit(solution)/shard_map/jit(_take)/gather | solution.py:33
  10.9 0.1 gather.19
  11.0 0.6 compare_select_fusion.6
  11.6 7.3 %all-to-all-start = ((s32[16,1,32]{2,1,0:T(1,128)}), s32[16,1,32]{2,1,0:T(1,128)S(1)}, u32[]{:S(2)}, u32[]{:S(2)}) async-start(s32[16,1,32]{2,1,0:T(1,128)} %get-tuple-element.10), calls=%async_computation | async-start | bytes 16384 | tf_op jit(solution)/shard_map/all_to_all | solution.py:37
  18.9 0.1 squeeze.9
  19.0 0.2 fusion.1
  19.2 0.1 fusion.2
  19.3 2.0 %gather_fusion.1 = bf16[512,768]{1,0:T(8,128)(2,1)S(1)} fusion(bf16[256,768]{1,0:T(8,128)(2,1)S(1)} %fusion.2, s32[1024]{0:T(1024)S(1)} %pad_clamp_fusion.1), kind=kCustom, calls=%fused_computation.1 | custom fusion | bytes 1574912 | tf_op jit(solution)/shard_map/jit(_take)/gather | solution.py:30
  21.4 1.0 broadcast_select_fusion
  22.4 2.3 %all-to-all-done = s32[16,1,32]{2,1,0:T(1,128)S(1)} async-done(((s32[16,1,32]{2,1,0:T(1,128)}), s32[16,1,32]{2,1,0:T(1,128)S(1)}, u32[]{:S(2)}, u32[]{:S(2)}) %all-to-all-start) | async-done | bytes 2080 | tf_op jit(solution)/shard_map/all_to_all | solution.py:37
  24.7 4.2 %all-to-all-start.2 = ((bf16[16,32,768]{2,1,0:T(8,128)(2,1)}), bf16[16,32,768]{2,1,0:T(8,128)(2,1)S(1)}, u32[]{:S(2)}, u32[]{:S(2)}) async-start(bf16[16,32,768]{2,1,0:T(8,128)(2,1)} %broadcast_select_fusion), calls=%async_computation.2 | async-start | bytes 1572864 | tf_op jit(solution)/shard_map/all_to_all | solution.py:36
  28.8 0.0 all-gather.4.cloned.1.call-start
  28.9 0.5 broadcast.392
  29.4 0.7 fusion.12
  30.1 0.1 reshape.333
  30.2 0.3 reduce-window.9
  30.5 0.1 slice.7
  30.6 0.1 reshape.331
  30.7 0.1 slice_reduce_fusion
  30.8 0.1 fusion.8
  30.9 18.0 %all-to-all-done.2 = bf16[16,32,768]{2,1,0:T(8,128)(2,1)S(1)} async-done(((bf16[16,32,768]{2,1,0:T(8,128)(2,1)}), bf16[16,32,768]{2,1,0:T(8,128)(2,1)S(1)}, u32[]{:S(2)}, u32[]{:S(2)}) %all-to-all-start.2) | async-done | bytes 786464 | tf_op jit(solution)/shard_map/all_to_all | solution.py:36
  48.8 1.1 convolution_convert_fusion
  50.0 0.0 all-gather.4.cloned.1.call-update
  50.0 4.5 %all-to-all-start.1 = ((s32[16,1,32]{2,1,0:T(1,128)}), s32[16,1,32]{2,1,0:T(1,128)S(1)}, u32[]{:S(2)}, u32[]{:S(2)}) async-start(s32[16,1,32]{2,1,0:T(1,128)} %get-tuple-element.9), calls=%async_computation.1 | async-start | bytes 16384 | tf_op jit(solution)/shard_map/all_to_all | solution.py:38
  54.5 0.1 reshape.328
  54.6 5.7 %all-to-all-done.1 = s32[16,1,32]{2,1,0:T(1,128)S(1)} async-done(((s32[16,1,32]{2,1,0:T(1,128)}), s32[16,1,32]{2,1,0:T(1,128)S(1)}, u32[]{:S(2)}, u32[]{:S(2)}) %all-to-all-start.1) | async-done | bytes 2080 | tf_op jit(solution)/shard_map/all_to_all | solution.py:38
  60.3 0.7 reduce.16
  61.0 0.1 broadcast_in_dim.73
  61.0 0.1 broadcast.355
  61.1 0.1 reshape.330
  61.2 0.3 select_reduce_fusion.1
  61.5 13.3 %all-gather = s32[8,1,256]{2,1,0:T(1,128)S(1)} all-gather(s32[1,1,256]{2,1,0:T(1,128)S(1)} %bitcast.34), channel_id=1, replica_groups=mesh['dom'=2,'bank'=2,'grp'=8] {'grp'}, dimensions={0}, use_global_device_ids=true | all-gather | bytes 9216 | tf_op jit(solution)/shard_map/all_gather | solution.py:57
  74.8 14.7 %all-gather.1 = s32[8,1,256]{2,1,0:T(1,128)S(1)} all-gather(s32[1,1,256]{2,1,0:T(1,128)S(1)} %bitcast.35), channel_id=1, replica_groups=mesh['dom'=2,'bank'=2,'grp'=8] {'grp'}, dimensions={0}, use_global_device_ids=true | all-gather | bytes 9216 | tf_op jit(solution)/shard_map/all_gather | solution.py:60
  89.5 18.9 %all-gather.4.cloned.1.call-done = bf16[2048,768]{1,0:T(8,128)(2,1)} async-done(((bf16[256,768]{1,0:T(8,128)(2,1)}), bf16[2048,768]{1,0:T(8,128)(2,1)}) %all-gather.4.cloned.1.call-update) | async-done | bytes 3145744 | tf_op jit(solution)/shard_map/all_gather | solution.py:56
  108.4 3.2 %fusion = f32[256]{0:T(256)S(1)} fusion(bf16[256,768]{1,0:T(8,128)(2,1)} %convolution_convert_fusion, bf16[2048,768]{1,0:T(8,128)(2,1)} %all-gather.4.cloned.1.call-done, s32[2048]{0:T(1024)S(1)} %bitcast.32, s32[2048]{0:T(1024)S(1)} %bitcast.31, s32[256]{0:T(256)S(1)} %get-tuple-element.8, s32[256]{0:T(256)S(1)} %get-tuple-element.7), kind=kOutput, calls=%fused_computation.5 | convolution fusion | flops 807927552 | bytes 3558400 | tf_op jit(solution)/shard_map/dot_general | solution.py:10
  111.6 3.5 %gather_fusion.2 = f32[512]{0:T(512)S(1)} fusion(f32[256]{0:T(256)S(1)} %broadcast_maximum_fusion, s32[1024]{0:T(1024)S(1)} %pad_clamp_fusion), kind=kCustom, calls=%fused_computation.2 | custom fusion | bytes 6144 | tf_op jit(solution)/shard_map/jit(_take)/gather | solution.py:64
  115.1 0.1 gather.23
  115.2 0.7 compare_select_fusion.9
  115.9 4.9 %all-to-all-start.3 = ((f32[16,1,32]{2,1,0:T(1,128)}), f32[16,1,32]{2,1,0:T(1,128)S(1)}, u32[]{:S(2)}, u32[]{:S(2)}) async-start(f32[16,1,32]{2,1,0:T(1,128)} %compare_select_fusion.9), calls=%async_computation.3 | async-start | bytes 16384 | tf_op jit(solution)/shard_map/all_to_all | solution.py:66
  120.8 0.1 ge.122
  120.8 5.7 %all-to-all-done.3 = f32[16,1,32]{2,1,0:T(1,128)S(1)} async-done(((f32[16,1,32]{2,1,0:T(1,128)}), f32[16,1,32]{2,1,0:T(1,128)S(1)}, u32[]{:S(2)}, u32[]{:S(2)}) %all-to-all-start.3) | async-done | bytes 2080 | tf_op jit(solution)/shard_map/all_to_all | solution.py:66
  126.5 0.5 broadcast.394
  127.0 0.7 reduce.17
  127.7 0.1 all_to_all.21
  127.8 4.6 %scatter_custom_fusion = f32[256]{0:T(256)} fusion(s32[512]{0:T(512)S(1)} %bitcast.29, f32[512]{0:T(512)S(1)} %broadcast_select_fusion.1, f32[]{:T(128)} %constant.30.clone.1), kind=kCustom, calls=%fused_computation.47 | custom fusion | flops 512 | bytes 1028 | tf_op jit(solution)/shard_map/scatter-max | solution.py:72
  (17 shorter events, 0.1 us)
Async XLA Ops:
  6.5 0.8 copy-start
  7.3 3.6 %copy-start.2 = (s32[1,16,32]{2,1,0:T(8,128)S(1)}, s32[1,16,32]{2,1,0:T(8,128)}, u32[]{:S(2)}) copy-start(s32[1,16,32]{2,1,0:T(8,128)} %param.5) | copy-start | bytes 6148
  7.4 11.7 %copy-start.1 = (bf16[256,768]{1,0:T(8,128)(2,1)S(1)}, bf16[256,768]{1,0:T(8,128)(2,1)}, u32[]{:S(2)}) copy-start(bf16[256,768]{1,0:T(8,128)(2,1)} %param.3) | copy-start | bytes 1179652
  11.6 13.1 %all-to-all-start = ((s32[16,1,32]{2,1,0:T(1,128)}), s32[16,1,32]{2,1,0:T(1,128)S(1)}, u32[]{:S(2)}, u32[]{:S(2)}) async-start(s32[16,1,32]{2,1,0:T(1,128)} %get-tuple-element.10), calls=%async_computation | async-start | bytes 16384 | tf_op jit(solution)/shard_map/all_to_all | solution.py:37
  24.7 24.1 %all-to-all-start.2 = ((bf16[16,32,768]{2,1,0:T(8,128)(2,1)}), bf16[16,32,768]{2,1,0:T(8,128)(2,1)S(1)}, u32[]{:S(2)}, u32[]{:S(2)}) async-start(bf16[16,32,768]{2,1,0:T(8,128)(2,1)} %broadcast_select_fusion), calls=%async_computation.2 | async-start | bytes 1572864 | tf_op jit(solution)/shard_map/all_to_all | solution.py:36
  28.8 79.5 %all-gather.4.cloned.1.call-start = ((), (), s32[]{:S(2)}) async-start(), calls=%async_computation.4 | async-start | bytes 3538944 | tf_op jit(solution)/shard_map/all_gather | solution.py:56
  50.0 10.3 %all-to-all-start.1 = ((s32[16,1,32]{2,1,0:T(1,128)}), s32[16,1,32]{2,1,0:T(1,128)S(1)}, u32[]{:S(2)}, u32[]{:S(2)}) async-start(s32[16,1,32]{2,1,0:T(1,128)} %get-tuple-element.9), calls=%async_computation.1 | async-start | bytes 16384 | tf_op jit(solution)/shard_map/all_to_all | solution.py:38
  115.9 10.6 %all-to-all-start.3 = ((f32[16,1,32]{2,1,0:T(1,128)}), f32[16,1,32]{2,1,0:T(1,128)S(1)}, u32[]{:S(2)}, u32[]{:S(2)}) async-start(f32[16,1,32]{2,1,0:T(1,128)} %compare_select_fusion.9), calls=%async_computation.3 | async-start | bytes 16384 | tf_op jit(solution)/shard_map/all_to_all | solution.py:66
Sparse Core Ops, SparseCore 0:
  50.1 58.2 all-gather.3
where the time goes:
time: 140 us; the launch traced here: 139 us
  waiting for transfers between devices  50.5 us (36%)
  blocking collectives  28 us (20%)
  starting transfers between devices  20.9 us (15%)
  between operations  13.5 us (10%)
  local copies, waits for them, and re-layouts  11.2 us (8%)
  other arithmetic  10.8 us (8%)
  matrix products  4.33 us (3%)
    all_gather x1, waiting for transfers between devices, on_device(): lax.all_gather(key_rows, 'grp', axis=0, tiled=True)  18.9 us
    all_to_all x1, waiting for transfers between devices, on_device(): lax.all_to_all(outgoing, ('bank', 'grp'), split_axis=0, concat_axis=0, ti...  18 us
    all_gather x1, blocking collectives, on_device(): lax.all_gather(key_crawl, 'grp', axis=0, tiled=True)[None, :]  14.7 us
    all_gather x1, blocking collectives, on_device(): lax.all_gather(key_cluster, 'grp', axis=0, tiled=True)  13.3 us
    all_to_all x1, starting transfers between devices, on_device(): lax.all_to_all(out_cluster, ('bank', 'grp'), split_axis=0, concat_axis=0,...  7.33 us
    all_to_all x1, waiting for transfers between devices, on_device(): lax.all_to_all(out_crawl, ('bank', 'grp'), split_axis=0, concat_axis=0, t...  5.7 us
    all_to_all x1, waiting for transfers between devices, on_device(): lax.all_to_all(slot_best, ('bank', 'grp'), split_axis=0, concat_axis=0, t...  5.68 us
    all_to_all x1, starting transfers between devices, on_device(): lax.all_to_all(slot_best, ('bank', 'grp'), split_axis=0, concat_axis=0, t...  4.86 us
  transfers between devices with their start and end apart: 5, of which 5 were waited for; matrix products, arithmetic and copies ran while one was open for 5% of the time, Pallas kernels for 0%

commit v1 on v0

--- a/solution.py
+++ b/solution.py
@@ -1,9 +1,13 @@
+import functools
 import jax
 import jax.numpy as jnp
 from jax import lax
+from jax.experimental import pallas as pl
+from jax.experimental.pallas import tpu as pltpu
 from jax.sharding import PartitionSpec as P
 
 small_eps = 1e-06
+MESH = pl.DeviceIdType.MESH
 
 
 def masked_scores(query_rows, query_cluster, other_rows, other_cluster):
@@ -14,7 +18,7 @@
     return (scores, matching)
 
 
-def on_device(embeddings, cluster_of, dest_list):
+def routed_on_device(embeddings, cluster_of, dest_list):
     rows_dev = embeddings.shape[0]
     width = embeddings.shape[1]
     devices_part = dest_list.shape[1]
@@ -74,9 +78,319 @@
     return result
 
 
+LOW = 8
+
+
+def pair_kernel(
+    emb_ref, cluster_ref, dest_ref, out_ref,
+    blocks, meta, columns, best, returned, own_meta,
+    block_send, meta_send, block_recv, meta_recv, best_send, best_recv,
+):
+    rows = emb_ref.shape[0]
+    n_dest = dest_ref.shape[0]
+    bank = lax.axis_index("bank")
+    grp = lax.axis_index("grp")
+    z = grp // 2
+    x = grp % 2
+    high = z // 2
+    inner_z = 1 + high
+    is_inner = z == inner_z
+    mine = 2 * x + bank
+    outer_add = jnp.where(is_inner, 0, 4)
+    own = mine + outer_add
+
+    barrier = pltpu.get_barrier_semaphore()
+    for b in range(2):
+        for g in range(8):
+
+            @pl.when((bank != b) | (grp != g))
+            def _():
+                pl.semaphore_signal(
+                    barrier, inc=1, device_id={"bank": b, "grp": g}, device_id_type=MESH
+                )
+
+    wide = emb_ref[...].astype(jnp.float32)
+    scale = lax.rsqrt(jnp.sum(wide * wide, axis=1, keepdims=True) + small_eps)
+    blocks[own] = (wide * scale).astype(jnp.bfloat16)
+
+    row_id = lax.broadcasted_iota(jnp.int32, (dest_ref.shape[1], rows), 1)
+    dest_columns = jnp.transpose(dest_ref[...].astype(jnp.float32)).astype(jnp.int32)
+    slab_wide = jnp.full(row_id.shape, -1, jnp.int32)
+    for d in range(n_dest):
+        named = dest_columns[:, d : d + 1] == row_id
+        slab_wide = jnp.maximum(slab_wide, jnp.where(named, d // (n_dest // 2), -1))
+    slab = jnp.max(slab_wide, axis=0, keepdims=True)
+    key = jnp.where(slab >= 0, cluster_ref[...] * 2 + slab, -1).astype(jnp.float32)
+    own_meta[...] = jnp.broadcast_to(key, own_meta.shape)
+    meta[own] = jnp.broadcast_to(key, own_meta.shape)
+    best[...] = jnp.full(best.shape, -1.0, jnp.float32)
+
+    pl.semaphore_wait(barrier, 15)
+
+    def send(index, slot, to_slot, to_bank, to_grp):
+        device = {"bank": to_bank, "grp": to_grp}
+        for buffer, sent, got in (
+            (meta, meta_send, meta_recv), (blocks, block_send, block_recv)
+        ):
+            pltpu.make_async_remote_copy(
+                src_ref=buffer.at[slot], dst_ref=buffer.at[to_slot],
+                send_sem=sent.at[index], recv_sem=got.at[to_slot],
+                device_id=device, device_id_type=MESH,
+            ).start()
+
+    def sent(index, slot):
+        for buffer, sem, got in (
+            (meta, meta_send, meta_recv), (blocks, block_send, block_recv)
+        ):
+            pltpu.make_async_remote_copy(
+                src_ref=buffer.at[slot], dst_ref=buffer.at[slot],
+                send_sem=sem.at[index], recv_sem=got.at[slot],
+                device_id={"bank": 1 - bank, "grp": grp}, device_id_type=MESH,
+            ).wait_send()
+
+    def arrive(slot):
+        for buffer, sem, got in (
+            (meta, meta_send, meta_recv), (blocks, block_send, block_recv)
+        ):
+            pltpu.make_async_remote_copy(
+                src_ref=buffer.at[slot], dst_ref=buffer.at[slot],
+                send_sem=sem.at[0], recv_sem=got.at[slot],
+                device_id={"bank": 1 - bank, "grp": grp}, device_id_type=MESH,
+            ).wait_recv()
+
+    def column(slot):
+        wide_key = jnp.broadcast_to(meta[slot][:1], (128, rows))
+        columns[slot] = jnp.transpose(wide_key)
+
+    def slot_of(rel, outer):
+        sx = (x + rel // 2) % 2
+        sb = (bank + rel % 2) % 2
+        slot = 2 * sx + sb + 4 * outer
+        sz = inner_z if outer == 0 else 3 * high
+        return slot, sb * 8 + sz * 2 + sx
+
+    def scores_into(k_slot, q_slot, diagonal):
+        s = lax.dot_general(
+            blocks[k_slot], blocks[q_slot], (((1,), (1,)), ((), ())),
+            preferred_element_type=jnp.float32,
+        )
+        k_key = columns[k_slot]
+        q_key = meta[q_slot][:1]
+        for h in range(rows // 128):
+            part = slice(h * 128, (h + 1) * 128)
+            allowed = k_key == q_key[:, part]
+            if diagonal:
+                k_id = lax.broadcasted_iota(jnp.int32, (rows, 128), 0)
+                q_id = lax.broadcasted_iota(jnp.int32, (rows, 128), 1) + h * 128
+                allowed = allowed & (k_id < q_id)
+            kept = jnp.where(allowed, s[:, part], -1.0)
+            top = jnp.max(kept.reshape(rows // 8, 8, 128), axis=0)
+            best[q_slot, :, part] = jnp.maximum(best[q_slot, :, part], top)
+
+    def earlier(k, q):
+        @pl.when(k[1] < q[1])
+        def _():
+            scores_into(k[0], q[0], False)
+
+    def low_pair(which, rel, outer):
+        slot, shard = slot_of(rel, outer)
+        swap = bank * (1 - (bank + rel % 2) % 2)
+        k_slot = (LOW + which) * (1 - swap) + slot * swap
+        q_slot = (LOW + which) * swap + slot * (1 - swap)
+        scores_into(k_slot, q_slot, False)
+
+    @pl.when(jnp.logical_not(is_inner))
+    def _():
+        send(0, own, own, bank, inner_z * 2 + x)
+
+    @pl.when(is_inner)
+    def _():
+        x_grp = z * 2 + (1 - x)
+        in0, in1, in2, in3 = (slot_of(r, 0) for r in range(4))
+        out0, out1, out2, out3 = (slot_of(r, 1) for r in range(4))
+
+        @pl.when(z == 1)
+        def _():
+            send(0, own, LOW, bank, grp + 2)
+
+        send(1, own, own, bank, x_grp)
+        send(2, own, own, 1 - bank, grp)
+        column(in0[0])
+        scores_into(in0[0], in0[0], True)
+        arrive(in1[0])
+        column(in1[0])
+        earlier(in1, in0)
+
+        arrive(out0[0])
+
+        @pl.when(z == 1)
+        def _():
+            send(3, out0[0], LOW + 1, bank, grp + 2)
+
+        send(4, out0[0], out0[0], bank, x_grp)
+        send(5, out0[0], out0[0], 1 - bank, grp)
+        arrive(in2[0])
+        send(6, in2[0], in2[0], 1 - bank, grp)
+        column(out0[0])
+        column(in2[0])
+        scores_into(out0[0], out0[0], True)
+        for k, q in ((out0, in0), (in0, out0), (in1, out0), (in2, in0), (in2, out0)):
+            earlier(k, q)
+        for k in (out1, in3):
+            arrive(k[0])
+            column(k[0])
+            earlier(k, in0)
+            earlier(k, out0)
+
+        @pl.when(z == 2)
+        def _():
+            arrive(LOW)
+            column(LOW)
+
+            @pl.loop(0, 4)
+            def _(rel):
+                low_pair(0, rel, 0)
+
+            @pl.loop(0, 2)
+            def _(rel):
+                low_pair(0, rel, 1)
+
+        arrive(out2[0])
+        send(7, out2[0], out2[0], 1 - bank, grp)
+        for k in (out2, out3):
+            if k is out3:
+                arrive(k[0])
+            column(k[0])
+            earlier(k, in0)
+            earlier(k, out0)
+
+        @pl.when(z == 2)
+        def _():
+            @pl.loop(2, 4)
+            def _(rel):
+                low_pair(0, rel, 1)
+
+            arrive(LOW + 1)
+            column(LOW + 1)
+
+            @pl.loop(0, 4)
+            def _(rel):
+                low_pair(1, rel, 0)
+
+            @pl.loop(0, 4)
+            def _(rel):
+                low_pair(1, rel, 1)
+
+    def best_copy(index, slot, to, to_bank, to_grp):
+        return pltpu.make_async_remote_copy(
+            src_ref=best.at[slot], dst_ref=returned.at[to],
+            send_sem=best_send.at[index], recv_sem=best_recv.at[to],
+            device_id={"bank": to_bank, "grp": to_grp}, device_id_type=MESH,
+        )
+
+    @pl.when(z == 1)
+    def _():
+        best_copy(0, mine + 4, 0, bank, grp - 2).start()
+
+    @pl.when(z == 2)
+    def _():
+        for rel in range(4):
+            slot, _ = slot_of(rel, 0)
+            to_bank = (bank + rel % 2) % 2
+            to_x = (x + rel // 2) % 2
+            best_copy(rel, slot + 4, mine, to_bank, 6 + to_x).start()
+            if rel:
+                best_copy(4 + rel, slot, mine, to_bank, 4 + to_x).start()
+
+        @pl.when(bank == 1)
+        def _():
+            best_copy(4, LOW, 1, bank, grp - 2).start()
+            best_copy(8, LOW + 1, 1, bank, grp - 4).start()
+
+    def take(index):
+        best_copy(0, own, index, 1 - bank, grp).wait_recv()
+        best[own] = jnp.maximum(best[own], returned[index])
+
+    def best_sent(index):
+        best_copy(index, own, 0, 1 - bank, grp).wait_send()
+
+    @pl.when(z == 0)
+    def _():
+        take(0)
+
+    @pl.when((z < 2) & (bank == 1))
+    def _():
+        take(1)
+
+    @pl.when(z >= 2)
+    def _():
+        for index in range(4):
+
+            @pl.when((z == 3) | (mine != index))
+            def _():
+                take(index)
+
+    top = jnp.max(best[own], axis=0, keepdims=True)
+    out_ref[...] = jnp.where(own_meta[:1] >= 0, top, -1.0)
+
+    @pl.when(jnp.logical_not(is_inner))
+    def _():
+        sent(0, own)
+
+    @pl.when(is_inner)
+    def _():
+        for index in (1, 2, 4, 5, 6, 7):
+            sent(index, own)
+
+    @pl.when(z == 1)
+    def _():
+        sent(0, own)
+        sent(3, own)
+        best_sent(0)
+
+    @pl.when(z == 2)
+    def _():
+        for index in (0, 1, 2, 3, 5, 6, 7):
+            best_sent(index)
+
+        @pl.when(bank == 1)
+        def _():
+            best_sent(4)
+            best_sent(8)
+
+
+def paired_on_device(embeddings, cluster_of, dest_list):
+    rows, width = embeddings.shape
+    dma = pltpu.SemaphoreType.DMA
+    vmem = pl.BlockSpec(memory_space=pltpu.VMEM)
+    result = pl.pallas_call(
+        pair_kernel,
+        out_shape=jax.ShapeDtypeStruct((1, rows), jnp.float32),
+        in_specs=[vmem] * 3,
+        out_specs=vmem,
+        scratch_shapes=[
+            pltpu.VMEM((10, rows, width), jnp.bfloat16),
+            pltpu.VMEM((10, 8, rows), jnp.float32),
+            pltpu.VMEM((10, rows, 128), jnp.float32),
+            pltpu.VMEM((10, 8, rows), jnp.float32),
+            pltpu.VMEM((4, 8, rows), jnp.float32),
+            pltpu.VMEM((8, rows), jnp.float32),
+            dma((8,)), dma((8,)), dma((10,)), dma((10,)), dma((9,)), dma((4,)),
+        ],
+        compiler_params=pltpu.CompilerParams(
+            collective_id=0, has_side_effects=True, vmem_limit_bytes=40 * 2**20
+        ),
+        cost_estimate=pl.CostEstimate(
+            flops=16 * 2 * rows * rows * width, bytes_accessed=rows * width * 2, transcendentals=rows
+        ),
+    )(embeddings, cluster_of.reshape(1, rows), dest_list[0])
+    return result.reshape(rows)
+
+
 def solution(mesh):
+    paired = mesh.shape["bank"] == 2 and mesh.shape["grp"] == 8
     return jax.shard_map(
-        on_device,
+        paired_on_device if paired else routed_on_device,
         mesh=mesh,
         in_specs=(
             P(("dom", "bank", "grp"), None),

time: 140 us -> 36.1 us (0.26)
  waiting for transfers between devices: 50.5 us -> 0 us
  Pallas kernels: 0 us -> 33 us
  blocking collectives: 28 us -> 0 us
  starting transfers between devices: 20.9 us -> 0 us
  between operations: 13.5 us -> 0.01 us
  other arithmetic: 10.8 us -> 0 us
  local copies, waits for them, and re-layouts: 11.2 us -> 2.93 us
  matrix products: 4.33 us -> 0 us
    pallas_call x0 -> x1, Pallas kernels: none -> 33 us  [paired_on_device(): pl.pallas_call(pair_kernel, out_shape=jax.ShapeDtypeStruct((1, rows), jnp...]
    all_to_all x4 -> x0, waiting for transfers between devices: 31.6 us -> none  [the longest x1 18 us: on_device(): lax.all_to_all(outgoing, ('bank', 'grp'), split_axis=0, concat_axis=0, ti...]
    all_gather x2 -> x0, blocking collectives: 28 us -> none  [the longest x1 14.7 us: on_device(): lax.all_gather(key_crawl, 'grp', axis=0, tiled=True)[None, :]]
    all_to_all x4 -> x0, starting transfers between devices: 20.9 us -> none  [the longest x1 7.33 us: on_device(): lax.all_to_all(out_cluster, ('bank', 'grp'), split_axis=0, concat_axis=0,...]
    all_gather x1 -> x0, waiting for transfers between devices: 18.9 us -> none  [on_device(): lax.all_gather(key_rows, 'grp', axis=0, tiled=True)]
    gather x5 -> x0, local copies, waits for them, and re-layouts: 9.19 us -> none  [the longest x2 3.58 us: on_device(): out_cluster = jnp.where(is_live, jnp.take(cluster_of, safe_rows), -1)]
    another operation x4 -> x0, other arithmetic: 4.99 us -> none  [the longest x1 4.64 us: on_device(): result = jnp.full((rows_dev,), -1.0, jnp.float32).at[safe_rows.reshape(-1...]
    dot_general x2 -> x0, matrix products: 4.33 us -> none  [the longest x1 3.21 us: masked_scores(): lax.dot_general(query_rows, other_rows, (((1,), (1,)), ((), ())), preferr...]
  transfers between devices with their start and end apart: 5 -> 0, of which waited for: 5 -> 0; matrix products, arithmetic and copies ran while one was open for 5% -> 0% of each run, Pallas kernels for 0% -> 0%
where the time goes in v1:
time: 36.1 us; the launch traced here: 35.9 us
  Pallas kernels  33 us (91%)
  local copies, waits for them, and re-layouts  2.93 us (8%)
    pallas_call x1, Pallas kernels, paired_on_device(): pl.pallas_call(pair_kernel, out_shape=jax.ShapeDtypeStruct((1, rows), jnp...  33 us
    unnamed x7, local copies, waits for them, and re-layouts  2.93 us

profile of v1, /device:TPU:1, one launch (start us, length us, event | category | flops | bytes accessed | tf_op | source)
XLA Modules:
  0.0 35.9 jit_solution(14216082195465752174)
XLA Ops:
  0.0 0.0 copy-start.2
  0.0 0.7 %copy-done.2 = s32[256]{0:T(256)S(1)} copy-done((s32[256]{0:T(256)S(1)}, s32[256]{0:T(256)}, u32[]{:S(2)}) %copy-start.2) | copy-done | bytes 1048
  0.7 0.0 copy-start
  0.7 1.0 %copy-done = bf16[256,768]{1,0:T(8,128)(2,1)S(1)} copy-done((bf16[256,768]{1,0:T(8,128)(2,1)S(1)}, bf16[256,768]{1,0:T(8,128)(2,1)}, u32[]{:S(2)}) %copy-start) | copy-done | bytes 393240
  1.7 0.0 copy-start.1
  1.7 0.7 %copy-done.1 = s32[1,16,32]{2,1,0:T(8,128)S(1)} copy-done((s32[1,16,32]{2,1,0:T(8,128)S(1)}, s32[1,16,32]{2,1,0:T(8,128)}, u32[]{:S(2)}) %copy-start.1) | copy-done | bytes 2072
  2.4 33.0 %shard_map.37 = f32[1,256]{1,0:T(1,128)S(1)} custom-call(bf16[256,768]{1,0:T(8,128)(2,1)S(1)} %copy-done, s32[1,256]{1,0:T(1,128)S(1)} %bitcast.5, s32[16,32]{1,0:T(8,128)S(1)} %bitcast.4), custom_call_target="tpu_custom_call" | custom-call | flops 1610612736 | bytes 393216 | tf_op jit(solution)/shard_map/pallas_call | solution.py:366
  35.4 0.6 %copy.5 = f32[256]{0:T(256)} copy(f32[256]{0:T(256)S(1)} %bitcast.3) | data formatting | bytes 2048
Async XLA Ops:
  0.0 0.7 %copy-start.2 = (s32[256]{0:T(256)S(1)}, s32[256]{0:T(256)}, u32[]{:S(2)}) copy-start(s32[256]{0:T(256)} %param.4) | copy-start | bytes 3076
  0.7 1.0 %copy-start = (bf16[256,768]{1,0:T(8,128)(2,1)S(1)}, bf16[256,768]{1,0:T(8,128)(2,1)}, u32[]{:S(2)}) copy-start(bf16[256,768]{1,0:T(8,128)(2,1)} %emb_ref.1) | copy-start | bytes 1179652
  1.7 0.7 %copy-start.1 = (s32[1,16,32]{2,1,0:T(8,128)S(1)}, s32[1,16,32]{2,1,0:T(8,128)}, u32[]{:S(2)}) copy-start(s32[1,16,32]{2,1,0:T(8,128)} %param.5) | copy-start | bytes 6148

commit v2 on v1

--- a/solution.py
+++ b/solution.py
@@ -82,11 +82,20 @@
 
 
 def pair_kernel(
-    emb_ref, cluster_ref, dest_ref, out_ref,
-    blocks, meta, columns, best, returned, own_meta,
-    block_send, meta_send, block_recv, meta_recv, best_send, best_recv,
+    emb_hbm, cluster_hbm, dest_hbm, out_ref,
+    emb_ref, cluster_ref, dest_ref, blocks, meta, columns, best, returned, own_meta,
+    load_sem, block_send, meta_send, block_recv, meta_recv, best_send, best_recv,
 ):
+    loads = [
+        pltpu.make_async_copy(source, target, load_sem.at[i])
+        for i, (source, target) in enumerate(
+            ((emb_hbm, emb_ref), (cluster_hbm, cluster_ref), (dest_hbm, dest_ref))
+        )
+    ]
+    for load in loads:
+        load.start()
     rows = emb_ref.shape[0]
+    half = rows // 2
     n_dest = dest_ref.shape[0]
     bank = lax.axis_index("bank")
     grp = lax.axis_index("grp")
@@ -109,10 +118,67 @@
                     barrier, inc=1, device_id={"bank": b, "grp": g}, device_id_type=MESH
                 )
 
+    loads[0].wait()
     wide = emb_ref[...].astype(jnp.float32)
     scale = lax.rsqrt(jnp.sum(wide * wide, axis=1, keepdims=True) + small_eps)
     blocks[own] = (wide * scale).astype(jnp.bfloat16)
 
+    pl.semaphore_wait(barrier, 15)
+
+    def block_copy(index, slot, to_slot, part, to_bank, to_grp):
+        span = pl.ds(part * half, half)
+        return pltpu.make_async_remote_copy(
+            src_ref=blocks.at[slot, span], dst_ref=blocks.at[to_slot, span],
+            send_sem=block_send.at[index, part], recv_sem=block_recv.at[to_slot, part],
+            device_id={"bank": to_bank, "grp": to_grp}, device_id_type=MESH,
+        )
+
+    def meta_copy(index, slot, to_slot, to_bank, to_grp):
+        return pltpu.make_async_remote_copy(
+            src_ref=meta.at[slot], dst_ref=meta.at[to_slot],
+            send_sem=meta_send.at[index], recv_sem=meta_recv.at[to_slot],
+            device_id={"bank": to_bank, "grp": to_grp}, device_id_type=MESH,
+        )
+
+    def sent(index, slot):
+        meta_copy(index, slot, slot, 1 - bank, grp).wait_send()
+        for part in range(2):
+            block_copy(index, slot, slot, part, 1 - bank, grp).wait_send()
+
+    def arrive_meta(slot):
+        meta_copy(0, slot, slot, 1 - bank, grp).wait_recv()
+
+    def arrive(slot, part):
+        block_copy(0, slot, slot, part, 1 - bank, grp).wait_recv()
+
+    def arrive_all(slot):
+        arrive_meta(slot)
+        arrive(slot, 0)
+        arrive(slot, 1)
+
+    x_grp = z * 2 + (1 - x)
+    partner = (1 - bank, grp)
+    beside = (bank, x_grp)
+
+    @pl.when(jnp.logical_not(is_inner))
+    def _():
+        for part in range(2):
+            block_copy(0, own, own, part, bank, inner_z * 2 + x).start()
+
+    @pl.when(z == 1)
+    def _():
+        for part in range(2):
+            block_copy(0, own, LOW, part, bank, grp + 2).start()
+
+    @pl.when(is_inner)
+    def _():
+        for part in range(2):
+            block_copy(1, own, own, part, *beside).start()
+        for part in range(2):
+            block_copy(2, own, own, part, *partner).start()
+
+    loads[1].wait()
+    loads[2].wait()
     row_id = lax.broadcasted_iota(jnp.int32, (dest_ref.shape[1], rows), 1)
     dest_columns = jnp.transpose(dest_ref[...].astype(jnp.float32)).astype(jnp.int32)
     slab_wide = jnp.full(row_id.shape, -1, jnp.int32)
@@ -125,38 +191,18 @@
     meta[own] = jnp.broadcast_to(key, own_meta.shape)
     best[...] = jnp.full(best.shape, -1.0, jnp.float32)
 
-    pl.semaphore_wait(barrier, 15)
-
-    def send(index, slot, to_slot, to_bank, to_grp):
-        device = {"bank": to_bank, "grp": to_grp}
-        for buffer, sent, got in (
-            (meta, meta_send, meta_recv), (blocks, block_send, block_recv)
-        ):
-            pltpu.make_async_remote_copy(
-                src_ref=buffer.at[slot], dst_ref=buffer.at[to_slot],
-                send_sem=sent.at[index], recv_sem=got.at[to_slot],
-                device_id=device, device_id_type=MESH,
-            ).start()
-
-    def sent(index, slot):
-        for buffer, sem, got in (
-            (meta, meta_send, meta_recv), (blocks, block_send, block_recv)
-        ):
-            pltpu.make_async_remote_copy(
-                src_ref=buffer.at[slot], dst_ref=buffer.at[slot],
-                send_sem=sem.at[index], recv_sem=got.at[slot],
-                device_id={"bank": 1 - bank, "grp": grp}, device_id_type=MESH,
-            ).wait_send()
-
-    def arrive(slot):
-        for buffer, sem, got in (
-            (meta, meta_send, meta_recv), (blocks, block_send, block_recv)
-        ):
-            pltpu.make_async_remote_copy(
-                src_ref=buffer.at[slot], dst_ref=buffer.at[slot],
-                send_sem=sem.at[0], recv_sem=got.at[slot],
-                device_id={"bank": 1 - bank, "grp": grp}, device_id_type=MESH,
-            ).wait_recv()
+    @pl.when(jnp.logical_not(is_inner))
+    def _():
+        meta_copy(0, own, own, bank, inner_z * 2 + x).start()
+
+    @pl.when(z == 1)
+    def _():
+        meta_copy(0, own, LOW, bank, grp + 2).start()
+
+    @pl.when(is_inner)
+    def _():
+        meta_copy(1, own, own, *beside).start()
+        meta_copy(2, own, own, *partner).start()
 
     def column(slot):
         wide_key = jnp.broadcast_to(meta[slot][:1], (128, rows))
@@ -169,22 +215,24 @@
         sz = inner_z if outer == 0 else 3 * high
         return slot, sb * 8 + sz * 2 + sx
 
-    def scores_into(k_slot, q_slot, diagonal):
+    def scores_into(k_slot, q_slot, diagonal, k_rows=slice(None), q_rows=slice(None)):
         s = lax.dot_general(
-            blocks[k_slot], blocks[q_slot], (((1,), (1,)), ((), ())),
+            blocks[k_slot, k_rows], blocks[q_slot, q_rows], (((1,), (1,)), ((), ())),
             preferred_element_type=jnp.float32,
         )
-        k_key = columns[k_slot]
+        k_key = columns[k_slot, k_rows]
         q_key = meta[q_slot][:1]
-        for h in range(rows // 128):
-            part = slice(h * 128, (h + 1) * 128)
+        first = q_rows.start or 0
+        for h in range(s.shape[1] // 128):
+            from_s = slice(h * 128, (h + 1) * 128)
+            part = slice(first + h * 128, first + (h + 1) * 128)
             allowed = k_key == q_key[:, part]
             if diagonal:
                 k_id = lax.broadcasted_iota(jnp.int32, (rows, 128), 0)
                 q_id = lax.broadcasted_iota(jnp.int32, (rows, 128), 1) + h * 128
                 allowed = allowed & (k_id < q_id)
-            kept = jnp.where(allowed, s[:, part], -1.0)
-            top = jnp.max(kept.reshape(rows // 8, 8, 128), axis=0)
+            kept = jnp.where(allowed, s[:, from_s], -1.0)
+            top = jnp.max(kept.reshape(s.shape[0] // 8, 8, 128), axis=0)
             best[q_slot, :, part] = jnp.maximum(best[q_slot, :, part], top)
 
     def earlier(k, q):
@@ -192,59 +240,71 @@
         def _():
             scores_into(k[0], q[0], False)
 
-    def low_pair(which, rel, outer):
+    def low_pair(which, rel, outer, part=None):
+        low = LOW + which
         slot, shard = slot_of(rel, outer)
-        swap = bank * (1 - (bank + rel % 2) % 2)
-        k_slot = (LOW + which) * (1 - swap) + slot * swap
-        q_slot = (LOW + which) * swap + slot * (1 - swap)
-        scores_into(k_slot, q_slot, False)
-
-    @pl.when(jnp.logical_not(is_inner))
-    def _():
-        send(0, own, own, bank, inner_z * 2 + x)
+        low_shard = bank * 8 + (1 - which) * 2 + x
+        if part is None:
+            low_rows = slice(None)
+        else:
+            low_rows = slice(part * half, (part + 1) * half)
+
+        @pl.when(low_shard < shard)
+        def _():
+            scores_into(low, slot, False, low_rows, slice(None))
+
+        @pl.when(low_shard > shard)
+        def _():
+            scores_into(slot, low, False, slice(None), low_rows)
 
     @pl.when(is_inner)
     def _():
-        x_grp = z * 2 + (1 - x)
         in0, in1, in2, in3 = (slot_of(r, 0) for r in range(4))
         out0, out1, out2, out3 = (slot_of(r, 1) for r in range(4))
-
-        @pl.when(z == 1)
-        def _():
-            send(0, own, LOW, bank, grp + 2)
-
-        send(1, own, own, bank, x_grp)
-        send(2, own, own, 1 - bank, grp)
         column(in0[0])
         scores_into(in0[0], in0[0], True)
-        arrive(in1[0])
+        arrive_all(in1[0])
         column(in1[0])
         earlier(in1, in0)
 
-        arrive(out0[0])
+        arrive_meta(out0[0])
 
         @pl.when(z == 1)
         def _():
-            send(3, out0[0], LOW + 1, bank, grp + 2)
-
-        send(4, out0[0], out0[0], bank, x_grp)
-        send(5, out0[0], out0[0], 1 - bank, grp)
-        arrive(in2[0])
-        send(6, in2[0], in2[0], 1 - bank, grp)
+            meta_copy(3, out0[0], LOW + 1, bank, grp + 2).start()
+
+        meta_copy(4, out0[0], out0[0], *beside).start()
+        meta_copy(5, out0[0], out0[0], *partner).start()
+        arrive_meta(in2[0])
+        meta_copy(6, in2[0], in2[0], *partner).start()
         column(out0[0])
         column(in2[0])
+        for part in range(2):
+            arrive(out0[0], part)
+
+            @pl.when(z == 1)
+            def _():
+                block_copy(3, out0[0], LOW + 1, part, bank, grp + 2).start()
+
+            block_copy(4, out0[0], out0[0], part, *beside).start()
+            block_copy(5, out0[0], out0[0], part, *partner).start()
+            arrive(in2[0], part)
+            block_copy(6, in2[0], in2[0], part, *partner).start()
+        arrive_meta(out2[0])
+        meta_copy(7, out2[0], out2[0], *partner).start()
+        column(out2[0])
         scores_into(out0[0], out0[0], True)
         for k, q in ((out0, in0), (in0, out0), (in1, out0), (in2, in0), (in2, out0)):
             earlier(k, q)
         for k in (out1, in3):
-            arrive(k[0])
+            arrive_all(k[0])
             column(k[0])
             earlier(k, in0)
             earlier(k, out0)
 
         @pl.when(z == 2)
         def _():
-            arrive(LOW)
+            arrive_all(LOW)
             column(LOW)
 
             @pl.loop(0, 4)
@@ -255,30 +315,35 @@
             def _(rel):
                 low_pair(0, rel, 1)
 
-        arrive(out2[0])
-        send(7, out2[0], out2[0], 1 - bank, grp)
-        for k in (out2, out3):
+            arrive_meta(LOW + 1)
+            column(LOW + 1)
+
+        for part in range(2):
+            arrive(out2[0], part)
+            block_copy(7, out2[0], out2[0], part, *partner).start()
+
+            @pl.when(z == 2)
+            def _():
+                arrive(LOW + 1, part)
+
+                @pl.loop(0, 4)
+                def _(rel):
+                    low_pair(1, rel, 0, part)
+
+                @pl.loop(0, 2)
+                def _(rel):
+                    low_pair(1, rel, 1, part)
+
+        for rel, k in ((2, out2), (3, out3)):
             if k is out3:
-                arrive(k[0])
-            column(k[0])
+                arrive_all(k[0])
+                column(k[0])
             earlier(k, in0)
             earlier(k, out0)
 
-        @pl.when(z == 2)
-        def _():
-            @pl.loop(2, 4)
-            def _(rel):
+            @pl.when(z == 2)
+            def _():
                 low_pair(0, rel, 1)
-
-            arrive(LOW + 1)
-            column(LOW + 1)
-
-            @pl.loop(0, 4)
-            def _(rel):
-                low_pair(1, rel, 0)
-
-            @pl.loop(0, 4)
-            def _(rel):
                 low_pair(1, rel, 1)
 
     def best_copy(index, slot, to, to_bank, to_grp):
@@ -366,16 +431,19 @@
     result = pl.pallas_call(
         pair_kernel,
         out_shape=jax.ShapeDtypeStruct((1, rows), jnp.float32),
-        in_specs=[vmem] * 3,
+        in_specs=[pl.BlockSpec(memory_space=pltpu.HBM)] * 3,
         out_specs=vmem,
         scratch_shapes=[
+            pltpu.VMEM((rows, width), jnp.bfloat16),
+            pltpu.VMEM((1, rows), jnp.int32),
+            pltpu.VMEM(dest_list.shape[1:], jnp.int32),
             pltpu.VMEM((10, rows, width), jnp.bfloat16),
             pltpu.VMEM((10, 8, rows), jnp.float32),
             pltpu.VMEM((10, rows, 128), jnp.float32),
             pltpu.VMEM((10, 8, rows), jnp.float32),
             pltpu.VMEM((4, 8, rows), jnp.float32),
             pltpu.VMEM((8, rows), jnp.float32),
-            dma((8,)), dma((8,)), dma((10,)), dma((10,)), dma((9,)), dma((4,)),
+            dma((3,)), dma((8, 2)), dma((8,)), dma((10, 2)), dma((10,)), dma((9,)), dma((4,)),
         ],
         compiler_params=pltpu.CompilerParams(
             collective_id=0, has_side_effects=True, vmem_limit_bytes=40 * 2**20

time: 36.1 us -> 35.9 us (level)
  no operation moved by 1% of the time
where the time goes in v2:
time: 35.9 us; the launch traced here: 35.7 us
  Pallas kernels  32.7 us (91%)
  local copies, waits for them, and re-layouts  2.93 us (8%)
    pallas_call x1, Pallas kernels, paired_on_device(): pl.pallas_call(pair_kernel, out_shape=jax.ShapeDtypeStruct((1, rows), jnp...  32.7 us
    unnamed x7, local copies, waits for them, and re-layouts  2.93 us

profile of v2, /device:TPU:1, one launch (start us, length us, event | category | flops | bytes accessed | tf_op | source)
XLA Modules:
  0.0 35.7 jit_solution(2423845170397738043)
XLA Ops:
  0.0 0.0 copy-start.2
  0.0 0.7 %copy-done.2 = s32[256]{0:T(256)S(1)} copy-done((s32[256]{0:T(256)S(1)}, s32[256]{0:T(256)}, u32[]{:S(2)}) %copy-start.2) | copy-done | bytes 1048
  0.7 0.0 copy-start
  0.7 1.0 %copy-done = bf16[256,768]{1,0:T(8,128)(2,1)S(1)} copy-done((bf16[256,768]{1,0:T(8,128)(2,1)S(1)}, bf16[256,768]{1,0:T(8,128)(2,1)}, u32[]{:S(2)}) %copy-start) | copy-done | bytes 393240
  1.7 0.0 copy-start.1
  1.7 0.7 %copy-done.1 = s32[1,16,32]{2,1,0:T(8,128)S(1)} copy-done((s32[1,16,32]{2,1,0:T(8,128)S(1)}, s32[1,16,32]{2,1,0:T(8,128)}, u32[]{:S(2)}) %copy-start.1) | copy-done | bytes 2072
  2.4 32.7 %shard_map.37 = f32[1,256]{1,0:T(1,128)S(1)} custom-call(bf16[256,768]{1,0:T(8,128)(2,1)S(1)} %copy-done, s32[1,256]{1,0:T(1,128)S(1)} %bitcast.5, s32[16,32]{1,0:T(8,128)S(1)} %bitcast.4), custom_call_target="tpu_custom_call" | custom-call | flops 1610612736 | bytes 393216 | tf_op jit(solution)/shard_map/pallas_call | solution.py:431
  35.1 0.6 %copy.5 = f32[256]{0:T(256)} copy(f32[256]{0:T(256)S(1)} %bitcast.3) | data formatting | bytes 2048
Async XLA Ops:
  0.0 0.7 %copy-start.2 = (s32[256]{0:T(256)S(1)}, s32[256]{0:T(256)}, u32[]{:S(2)}) copy-start(s32[256]{0:T(256)} %param.4) | copy-start | bytes 3076
  0.7 1.0 %copy-start = (bf16[256,768]{1,0:T(8,128)(2,1)S(1)}, bf16[256,768]{1,0:T(8,128)(2,1)}, u32[]{:S(2)}) copy-start(bf16[256,768]{1,0:T(8,128)(2,1)} %emb_hbm.1) | copy-start | bytes 1179652
  1.7 0.7 %copy-start.1 = (s32[1,16,32]{2,1,0:T(8,128)S(1)}, s32[1,16,32]{2,1,0:T(8,128)}, u32[]{:S(2)}) copy-start(s32[1,16,32]{2,1,0:T(8,128)} %param.5) | copy-start | bytes 6148

commit v3 on v2

--- a/solution.py
+++ b/solution.py
@@ -84,7 +84,7 @@
 def pair_kernel(
     emb_hbm, cluster_hbm, dest_hbm, out_ref,
     emb_ref, cluster_ref, dest_ref, blocks, meta, columns, best, returned, own_meta,
-    load_sem, block_send, meta_send, block_recv, meta_recv, best_send, best_recv,
+    load_sem, ready_sem, block_send, meta_send, block_recv, meta_recv, best_send, best_recv,
 ):
     loads = [
         pltpu.make_async_copy(source, target, load_sem.at[i])
@@ -109,21 +109,70 @@
     own = mine + outer_add
 
     barrier = pltpu.get_barrier_semaphore()
-    for b in range(2):
-        for g in range(8):
-
-            @pl.when((bank != b) | (grp != g))
-            def _():
-                pl.semaphore_signal(
-                    barrier, inc=1, device_id={"bank": b, "grp": g}, device_id_type=MESH
-                )
+    x_grp = z * 2 + (1 - x)
+    partner = (1 - bank, grp)
+    beside = (bank, x_grp)
+
+    def greet(to_bank, to_grp, sem=barrier):
+        pl.semaphore_signal(
+            sem, inc=1, device_id={"bank": to_bank, "grp": to_grp}, device_id_type=MESH
+        )
+
+    greet(*beside)
+
+    @pl.when(z == 0)
+    def _():
+        greet(bank, grp + 2)
+
+    @pl.when((z == 0) & (bank == 1))
+    def _():
+        greet(bank, grp + 4)
+
+    @pl.when(z == 1)
+    def _():
+        greet(*partner)
+        greet(bank, grp - 2)
+
+    @pl.when((z == 1) & (bank == 1))
+    def _():
+        greet(bank, grp + 2)
+
+    @pl.when(z == 2)
+    def _():
+        greet(*partner)
+        greet(1 - bank, x_grp)
+        greet(bank, grp - 2)
+        for b in range(2):
+            for other_x in range(2):
+                greet(b, 6 + other_x)
 
     loads[0].wait()
     wide = emb_ref[...].astype(jnp.float32)
     scale = lax.rsqrt(jnp.sum(wide * wide, axis=1, keepdims=True) + small_eps)
     blocks[own] = (wide * scale).astype(jnp.bfloat16)
 
-    pl.semaphore_wait(barrier, 15)
+    @pl.when(z == 0)
+    def _():
+        pl.semaphore_wait(barrier, 2)
+
+    @pl.when(z == 1)
+    def _():
+        pl.semaphore_wait(barrier, 4)
+
+    @pl.when((z == 2) & (bank == 0))
+    def _():
+        pl.semaphore_wait(barrier, 3)
+
+    @pl.when((z == 2) & (bank == 1))
+    def _():
+        pl.semaphore_wait(barrier, 5)
+
+    @pl.when(z == 3)
+    def _():
+        pl.semaphore_wait(barrier, 5)
+        for b in range(2):
+            for other_x in range(2):
+                greet(b, 4 + other_x, ready_sem)
 
     def block_copy(index, slot, to_slot, part, to_bank, to_grp):
         span = pl.ds(part * half, half)
@@ -140,9 +189,10 @@
             device_id={"bank": to_bank, "grp": to_grp}, device_id_type=MESH,
         )
 
-    def sent(index, slot):
-        meta_copy(index, slot, slot, 1 - bank, grp).wait_send()
-        for part in range(2):
+    def sent(index, slot, parts=(0, 1), with_meta=True):
+        if with_meta:
+            meta_copy(index, slot, slot, 1 - bank, grp).wait_send()
+        for part in parts:
             block_copy(index, slot, slot, part, 1 - bank, grp).wait_send()
 
     def arrive_meta(slot):
@@ -156,14 +206,11 @@
         arrive(slot, 0)
         arrive(slot, 1)
 
-    x_grp = z * 2 + (1 - x)
-    partner = (1 - bank, grp)
-    beside = (bank, x_grp)
-
     @pl.when(jnp.logical_not(is_inner))
     def _():
         for part in range(2):
             block_copy(0, own, own, part, bank, inner_z * 2 + x).start()
+        block_copy(1, own, own, 1, *beside).start()
 
     @pl.when(z == 1)
     def _():
@@ -286,7 +333,8 @@
             def _():
                 block_copy(3, out0[0], LOW + 1, part, bank, grp + 2).start()
 
-            block_copy(4, out0[0], out0[0], part, *beside).start()
+            if part == 0:
+                block_copy(4, out0[0], out0[0], part, *beside).start()
             block_copy(5, out0[0], out0[0], part, *partner).start()
             arrive(in2[0], part)
             block_copy(6, in2[0], in2[0], part, *partner).start()
@@ -346,6 +394,12 @@
                 low_pair(0, rel, 1)
                 low_pair(1, rel, 1)
 
+    @pl.when(jnp.logical_not(is_inner))
+    def _():
+        other = 2 * (1 - x) + bank + 4
+        arrive(other, 1)
+        block_copy(2, other, other, 1, bank, inner_z * 2 + x).start()
+
     def best_copy(index, slot, to, to_bank, to_grp):
         return pltpu.make_async_remote_copy(
             src_ref=best.at[slot], dst_ref=returned.at[to],
@@ -359,6 +413,7 @@
 
     @pl.when(z == 2)
     def _():
+        pl.semaphore_wait(ready_sem, 4)
         for rel in range(4):
             slot, _ = slot_of(rel, 0)
             to_bank = (bank + rel % 2) % 2
@@ -401,11 +456,14 @@
     @pl.when(jnp.logical_not(is_inner))
     def _():
         sent(0, own)
+        for index in (1, 2):
+            sent(index, own, (1,), False)
 
     @pl.when(is_inner)
     def _():
-        for index in (1, 2, 4, 5, 6, 7):
+        for index in (1, 2, 5, 6, 7):
             sent(index, own)
+        sent(4, own, (0,))
 
     @pl.when(z == 1)
     def _():
@@ -443,10 +501,10 @@
             pltpu.VMEM((10, 8, rows), jnp.float32),
             pltpu.VMEM((4, 8, rows), jnp.float32),
             pltpu.VMEM((8, rows), jnp.float32),
-            dma((3,)), dma((8, 2)), dma((8,)), dma((10, 2)), dma((10,)), dma((9,)), dma((4,)),
+            dma((3,)), pltpu.SemaphoreType.REGULAR, dma((8, 2)), dma((8,)), dma((10, 2)), dma((10,)), dma((9,)), dma((4,)),
         ],
         compiler_params=pltpu.CompilerParams(
-            collective_id=0, has_side_effects=True, vmem_limit_bytes=40 * 2**20
+            collective_id=0, has_side_effects=True, vmem_limit_bytes=60 * 2**20
         ),
         cost_estimate=pl.CostEstimate(
             flops=16 * 2 * rows * rows * width, bytes_accessed=rows * width * 2, transcendentals=rows

time: 35.9 us -> 31.7 us (0.88)
  Pallas kernels: 32.7 us -> 30.3 us
  local copies, waits for them, and re-layouts: 2.93 us -> 1.22 us
    pallas_call x1, Pallas kernels: 32.7 us -> 30.3 us  [paired_on_device(): pl.pallas_call(pair_kernel, out_shape=jax.ShapeDtypeStruct((1, rows), jnp...]
    unnamed x7 -> x3, local copies, waits for them, and re-layouts: 2.93 us -> 1.22 us
where the time goes in v3:
time: 31.7 us; the launch traced here: 31.6 us
  Pallas kernels  30.3 us (96%)
  local copies, waits for them, and re-layouts  1.22 us (4%)
    pallas_call x1, Pallas kernels, paired_on_device(): pl.pallas_call(pair_kernel, out_shape=jax.ShapeDtypeStruct((1, rows), jnp...  30.3 us
    unnamed x3, local copies, waits for them, and re-layouts  1.22 us

profile of v3, /device:TPU:1, one launch (start us, length us, event | category | flops | bytes accessed | tf_op | source)
XLA Modules:
  0.0 31.6 jit_solution(16612485173431604687)
XLA Ops:
  0.0 30.3 %shard_map.37 = f32[1,256]{1,0:T(1,128)} custom-call(bf16[256,768]{1,0:T(8,128)(2,1)} %emb_hbm.1, s32[1,256]{1,0:T(1,128)} %bitcast.5, s32[16,32]{1,0:T(8,128)} %bitcast.4), custom_call_target="tpu_custom_call" | custom-call | flops 1610612736 | bytes 393216 | tf_op jit(solution)/shard_map/pallas_call | solution.py:489
  30.3 0.0 copy-start
  30.3 0.7 %copy-done = f32[1,256]{1,0:T(1,128)S(1)} copy-done((f32[1,256]{1,0:T(1,128)S(1)}, f32[1,256]{1,0:T(1,128)}, u32[]{:S(2)}) %copy-start) | copy-done | bytes 1048
  31.0 0.6 %copy.5 = f32[256]{0:T(256)} copy(f32[256]{0:T(256)S(1)} %bitcast.3) | data formatting | bytes 2048
Async XLA Ops:
  30.3 0.7 %copy-start = (f32[1,256]{1,0:T(1,128)S(1)}, f32[1,256]{1,0:T(1,128)}, u32[]{:S(2)}) copy-start(f32[1,256]{1,0:T(1,128)} %shard_map.37) | copy-start | bytes 3076

commit v4 on v3

--- a/solution.py
+++ b/solution.py
@@ -370,17 +370,18 @@
             arrive(out2[0], part)
             block_copy(7, out2[0], out2[0], part, *partner).start()
 
-            @pl.when(z == 2)
-            def _():
+        @pl.when(z == 2)
+        def _():
+            for part in range(2):
                 arrive(LOW + 1, part)
 
-                @pl.loop(0, 4)
-                def _(rel):
-                    low_pair(1, rel, 0, part)
-
-                @pl.loop(0, 2)
-                def _(rel):
-                    low_pair(1, rel, 1, part)
+            @pl.loop(0, 4)
+            def _(rel):
+                low_pair(1, rel, 0)
+
+            @pl.loop(0, 2)
+            def _(rel):
+                low_pair(1, rel, 1)
 
         for rel, k in ((2, out2), (3, out3)):
             if k is out3:

time: 31.7 us -> 30.4 us (0.959)
  Pallas kernels: 30.3 us -> 29 us
    pallas_call x1, Pallas kernels: 30.3 us -> 29 us  [paired_on_device(): pl.pallas_call(pair_kernel, out_shape=jax.ShapeDtypeStruct((1, rows), jnp...]
where the time goes in v4:
time: 30.4 us; the launch traced here: 30.2 us
  Pallas kernels  29 us (95%)
  local copies, waits for them, and re-layouts  1.22 us (4%)
    pallas_call x1, Pallas kernels, paired_on_device(): pl.pallas_call(pair_kernel, out_shape=jax.ShapeDtypeStruct((1, rows), jnp...  29 us
    unnamed x3, local copies, waits for them, and re-layouts  1.22 us

profile of v4, /device:TPU:1, one launch (start us, length us, event | category | flops | bytes accessed | tf_op | source)
XLA Modules:
  0.0 30.2 jit_solution(15539022514977209202)
XLA Ops:
  0.0 29.0 %shard_map.37 = f32[1,256]{1,0:T(1,128)} custom-call(bf16[256,768]{1,0:T(8,128)(2,1)} %emb_hbm.1, s32[1,256]{1,0:T(1,128)} %bitcast.5, s32[16,32]{1,0:T(8,128)} %bitcast.4), custom_call_target="tpu_custom_call" | custom-call | flops 1610612736 | bytes 393216 | tf_op jit(solution)/shard_map/pallas_call | solution.py:490
  29.0 0.0 copy-start
  29.0 0.7 %copy-done = f32[1,256]{1,0:T(1,128)S(1)} copy-done((f32[1,256]{1,0:T(1,128)S(1)}, f32[1,256]{1,0:T(1,128)}, u32[]{:S(2)}) %copy-start) | copy-done | bytes 1048
  29.7 0.6 %copy.5 = f32[256]{0:T(256)} copy(f32[256]{0:T(256)S(1)} %bitcast.3) | data formatting | bytes 2048
Async XLA Ops:
  29.0 0.7 %copy-start = (f32[1,256]{1,0:T(1,128)S(1)}, f32[1,256]{1,0:T(1,128)}, u32[]{:S(2)}) copy-start(f32[1,256]{1,0:T(1,128)} %shard_map.37) | copy-start | bytes 3076

commit v5 on v4

--- a/solution.py
+++ b/solution.py
@@ -359,16 +359,19 @@
             def _(rel):
                 low_pair(0, rel, 0)
 
+
+        for part in range(2):
+            arrive(out2[0], part)
+            block_copy(7, out2[0], out2[0], part, *partner).start()
+
+        @pl.when(z == 2)
+        def _():
             @pl.loop(0, 2)
             def _(rel):
                 low_pair(0, rel, 1)
 
             arrive_meta(LOW + 1)
             column(LOW + 1)
-
-        for part in range(2):
-            arrive(out2[0], part)
-            block_copy(7, out2[0], out2[0], part, *partner).start()
 
         @pl.when(z == 2)
         def _():

time: 30.4 us -> 30.4 us (level)
  no operation moved by 1% of the time
where the time goes in v5:
time: 30.4 us; the launch traced here: 30.2 us
  Pallas kernels  29 us (95%)
  local copies, waits for them, and re-layouts  1.22 us (4%)
    pallas_call x1, Pallas kernels, paired_on_device(): pl.pallas_call(pair_kernel, out_shape=jax.ShapeDtypeStruct((1, rows), jnp...  29 us
    unnamed x3, local copies, waits for them, and re-layouts  1.22 us

profile of v5, /device:TPU:1, one launch (start us, length us, event | category | flops | bytes accessed | tf_op | source)
XLA Modules:
  0.0 30.2 jit_solution(10800964276839240962)
XLA Ops:
  0.0 29.0 %shard_map.37 = f32[1,256]{1,0:T(1,128)} custom-call(bf16[256,768]{1,0:T(8,128)(2,1)} %emb_hbm.1, s32[1,256]{1,0:T(1,128)} %bitcast.5, s32[16,32]{1,0:T(8,128)} %bitcast.4), custom_call_target="tpu_custom_call" | custom-call | flops 1610612736 | bytes 393216 | tf_op jit(solution)/shard_map/pallas_call | solution.py:493
  29.0 0.0 copy-start
  29.0 0.7 %copy-done = f32[1,256]{1,0:T(1,128)S(1)} copy-done((f32[1,256]{1,0:T(1,128)S(1)}, f32[1,256]{1,0:T(1,128)}, u32[]{:S(2)}) %copy-start) | copy-done | bytes 1048
  29.7 0.6 %copy.5 = f32[256]{0:T(256)} copy(f32[256]{0:T(256)S(1)} %bitcast.3) | data formatting | bytes 2048
Async XLA Ops:
  29.0 0.7 %copy-start = (f32[1,256]{1,0:T(1,128)S(1)}, f32[1,256]{1,0:T(1,128)}, u32[]{:S(2)}) copy-start(f32[1,256]{1,0:T(1,128)} %shard_map.37) | copy-start | bytes 3076
